TPU v7x, 128 devices: a whole 4x4x4 slice. The times are simulated.
128 devices in a mesh: seq: 16 (over z, y), expert: 8 (over x, core).
Axes of the slice: x: 4, y: 4, z: 4, core: 2. Of those that a mesh axis runs over, the one named last changes fastest.
Arguments:
- tokens: bfloat16 [2048, 4096], P(('seq', 'expert')), may hold values from -6 to 6
- gain_mamba: float32 [4096], replicated, may hold values from 0.1 to 1.9
- in_weight: bfloat16 [2, 4096, 8192], P(None, 'seq', 'expert'), may hold values from -0.09375 to 0.09375
- conv_weight: float32 [4, 8192], P(None, 'expert'), may hold values from -3 to 3
- conv_bias: float32 [8192], P('expert'), may hold values from -3 to 3
- xproj_weight: bfloat16 [8192, 288], P('expert'), may hold values from -0.0625 to 0.0625
- dt_weight: bfloat16 [256, 8192], P(None, 'expert'), may hold values from -0.375 to 0.375
- dt_bias: float32 [8192], P('expert'), may hold values from -7 to -2
- a_rate: float32 [16, 8192], P(None, 'expert'), may hold values from 0.01 to 8
- skip_d: float32 [8192], P('expert'), may hold values from 0.5 to 1.5
- out_weight: bfloat16 [8192, 4096], P('expert', 'seq'), may hold values from -0.0625 to 0.0625
- gain_moe: float32 [4096], replicated, may hold values from 0.1 to 1.9
- expert_ids: int32 [2048, 2], P(('seq', 'expert')), may hold values from 0 to 15, all different within a row; in each aligned block of 16 rows (0 to 15, 16 to 31, ...) at most 4 rows name the same one
- gate_weights: float32 [2048, 2], P(('seq', 'expert')), may hold values from 0.2 to 1
- w_gate: bfloat16 [16, 4096, 7168], P('seq', None, 'expert'), may hold values from -0.09375 to 0.09375
- w_up: bfloat16 [16, 4096, 7168], P('seq', None, 'expert'), may hold values from -0.09375 to 0.09375
- w_down: bfloat16 [16, 7168, 4096], P('seq', 'expert'), may hold values from -0.0625 to 0.0625
Outputs:
- mixed: bfloat16 [2048, 4096], P(('seq', 'expert'))
Inputs may be any that keep to these rules, and one draw needn't show every extreme that they name: `expert_ids`: each row names 2 different experts. In each aligned block of 16 rows (the rows of one device) no expert is named by more than 4 rows, a bound that some block reaches.
All inputs are finite; a program needn't handle non-finite values.
Results may differ from a plain program's by a relative error of at most 0.03.
Values may be sent and summed in bfloat16 or wider, within the bound.
A program may use at most 192 MiB of HBM per device.

v0:
```python
import jax
import jax.numpy as jnp
from jax import lax
from jax.sharding import PartitionSpec as P

STATE = 16
CONV = 4
RANK = 256
TOP = 2


def from_behind(block, axis, distance):
    devices = range(lax.axis_size(axis))
    route = [(i - distance, i) for i in devices if i - distance in devices]
    return lax.ppermute(block, axis, route)


def rms_norm(values, gain):
    wide = values.astype(jnp.float32)
    return wide * lax.rsqrt(jnp.mean(wide * wide, axis=-1, keepdims=True) + 1e-05) * gain


def combine_states(earlier, later):
    return (earlier[0] * later[0], later[0] * earlier[1] + later[1])


def per_device(
    tokens,
    gain_mamba,
    in_weight,
    conv_weight,
    conv_bias,
    xproj_weight,
    dt_weight,
    dt_bias,
    a_rate,
    skip_d,
    out_weight,
    gain_moe,
    expert_ids,
    gate_weights,
    w_gate,
    w_up,
    w_down,
):
    rows, dim = tokens.shape
    n_seq = lax.axis_size("seq")
    n_exp = lax.axis_size("expert")
    group = lax.all_gather(tokens, "expert", axis=0, tiled=True)
    local_tok = group.shape[0]
    normed = rms_norm(group, gain_mamba).astype(jnp.bfloat16)
    both = jnp.einsum(
        "td,kdc->tkc",
        normed,
        lax.all_gather(in_weight, "seq", axis=1, tiled=True),
        preferred_element_type=jnp.float32,
    )
    xpart = both[:, 0]
    zpart = both[:, 1]
    edge = from_behind(xpart[local_tok - (CONV - 1) :], "seq", 1)
    padded = jnp.concatenate([edge, xpart], axis=0)
    conv = conv_bias
    for tap in range(CONV):
        conv = conv + conv_weight[tap] * padded[tap : tap + local_tok]
    inner = jax.nn.silu(conv).astype(jnp.bfloat16)
    partial_value = jnp.dot(inner, xproj_weight, preferred_element_type=jnp.float32)
    low_part, edge_part = (
        lax.psum(partial_value[:, :RANK].astype(jnp.bfloat16), "expert").astype(jnp.float32),
        lax.psum(partial_value[:, RANK:].astype(jnp.bfloat16), "expert").astype(jnp.float32),
    )
    dt_low = low_part.astype(jnp.bfloat16)
    bmat = edge_part[:, :STATE]
    cmat = edge_part[:, STATE:]
    step = jax.nn.softplus(jnp.dot(dt_low, dt_weight, preferred_element_type=jnp.float32) + dt_bias)
    inner_f = inner.astype(jnp.float32)
    decay = jnp.exp(-step[:, None, :] * a_rate[None, :, :])
    source = bmat[:, :, None] * (step * inner_f)[:, None, :]
    cumulative, states = lax.associative_scan(combine_states, (decay, source), axis=0)
    total = cumulative[-1]
    final = states[-1]

    def relay(turn, incoming):
        return from_behind((total * incoming + final).astype(jnp.bfloat16), "seq", 1).astype(
            jnp.float32
        )

    arriving = lax.fori_loop(0, n_seq - 1, relay, jnp.zeros_like(final))
    states = states + cumulative * arriving[None, :, :]
    readout = jnp.sum(cmat[:, :, None] * states, axis=1)
    gated = ((readout + skip_d * inner_f) * jax.nn.silu(zpart)).astype(jnp.bfloat16)
    terms = jnp.dot(
        gated,
        lax.all_gather(out_weight, "seq", axis=1, tiled=True),
        preferred_element_type=jnp.float32,
    )
    mixer = lax.psum_scatter(
        terms.astype(jnp.bfloat16), "expert", scatter_dimension=0, tiled=True
    ).astype(jnp.float32)
    resid = (tokens.astype(jnp.float32) + mixer).astype(jnp.bfloat16)
    normed2 = rms_norm(resid, gain_moe).astype(jnp.bfloat16)
    capacity = max(2, 4 * rows // n_seq)
    slots_all = n_seq * capacity
    flat_ids = expert_ids.reshape(-1)
    onehot = (flat_ids[:, None] == jnp.arange(n_seq, dtype=jnp.int32)[None, :]).astype(jnp.int32)
    before = jnp.cumsum(onehot, axis=0) - onehot
    slot = jnp.sum(before * onehot, axis=1)
    target = flat_ids * capacity + slot
    places = target[:, None] == jnp.arange(slots_all, dtype=jnp.int32)[None, :]
    dispatch_mat = jnp.any(places.reshape(rows, TOP, slots_all), axis=1).astype(jnp.bfloat16)
    send = jnp.einsum(
        "rp,rd->pd", dispatch_mat, normed2, preferred_element_type=jnp.float32
    ).astype(jnp.bfloat16)
    received = lax.all_to_all(
        send.reshape(n_seq, capacity, dim), "seq", split_axis=0, concat_axis=0, tiled=True
    )
    pooled = lax.all_gather(
        received.reshape(1, slots_all, dim), "expert", axis=0, tiled=True
    ).reshape(n_exp * slots_all, dim)
    gate = jnp.dot(pooled, w_gate[0], preferred_element_type=jnp.float32)
    upper = jnp.dot(pooled, w_up[0], preferred_element_type=jnp.float32)
    act = (jax.nn.silu(gate) * upper).astype(jnp.bfloat16)
    outputs = lax.psum_scatter(
        jnp.dot(act, w_down[0], preferred_element_type=jnp.float32).astype(jnp.bfloat16),
        "expert",
        scatter_dimension=0,
        tiled=True,
    )
    returned = lax.all_to_all(
        outputs.reshape(n_seq, capacity, dim), "seq", split_axis=0, concat_axis=0, tiled=True
    ).reshape(slots_all, dim)
    weighting = jnp.where(places, gate_weights.reshape(-1)[:, None], 0.0)
    weighting = jnp.sum(weighting.reshape(rows, TOP, slots_all), axis=1)
    moe = jnp.dot(weighting, returned.astype(jnp.float32), precision=lax.Precision.HIGHEST)
    return (resid.astype(jnp.float32) + moe).astype(jnp.bfloat16)


def solution(mesh):
    placed = (
        P(("seq", "expert"), None),
        P(),
        P(None, "seq", "expert"),
        P(None, "expert"),
        P("expert"),
        P("expert", None),
        P(None, "expert"),
        P("expert"),
        P(None, "expert"),
        P("expert"),
        P("expert", "seq"),
        P(),
        P(("seq", "expert"), None),
        P(("seq", "expert"), None),
        P("seq", None, "expert"),
        P("seq", None, "expert"),
        P("seq", "expert", None),
    )
    return jax.shard_map(
        per_device,
        mesh=mesh,
        in_specs=placed,
        out_specs=P(("seq", "expert"), None),
        check_vma=False,
    )
```

profile of v0, /device:TPU:0, one launch (start us, length us, event | category | flops | bytes accessed | tf_op | source)
XLA Modules:
  0.0 908.5 jit_solution(7577490913799089768)
XLA Ops:
  8.9 26.0 %all-gather.5.cloned.1.call-done = bf16[128,4096]{1,0:T(8,128)(2,1)} async-done(((bf16[16,4096]{1,0:T(8,128)(2,1)}), bf16[128,4096]{1,0:T(8,128)(2,1)}) %all-gather.5.cloned.1.call-update) | async-done | bytes 1048592 | tf_op jit(solution)/shard_map/all_gather | solution.py:49
  36.5 111.9 %all-gather.7.cloned.1.call-done = bf16[2,4096,1024]{2,1,0:T(8,128)(2,1)} async-done(((bf16[2,256,1024]{2,1,0:T(8,128)(2,1)}), bf16[2,4096,1024]{2,1,0:T(8,128)(2,1)}) %all-gather.7.cloned.1.call-update) | async-done | bytes 16777232 | tf_op jit(solution)/shard_map/all_gather | solution.py:55
  148.4 8.5 fusion.20
  163.9 14.0 %psum.14 = bf16[128,32]{0,1:T(8,128)(2,1)S(1)} all-reduce(bf16[128,32]{0,1:T(8,128)(2,1)S(1)} %slice.341), channel_id=1, replica_groups=mesh['seq'=16,'expert'=8] {'expert'}, use_global_device_ids=true, to_apply=%region_1.2 | all-reduce | flops 4096 | bytes 16384 | tf_op jit(solution)/shard_map/psum | solution.py:69
  178.7 44.8 %all-reduce.30.cloned.1.call-done = bf16[128,256]{0,1:T(8,128)(2,1)} async-done(((bf16[128,256]{0,1:T(8,128)(2,1)}), bf16[128,256]{0,1:T(8,128)(2,1)}) %all-reduce.30.cloned.1.call-update) | async-done | bytes 65552 | tf_op jit(solution)/shard_map/psum | solution.py:68
  233.5 10.9 %slice_add_fusion = (f32[64,16,1024]{2,1,0:T(8,128)S(1)}, f32[64,16,1024]{2,1,0:T(8,128)}) fusion(f32[128,16,1024]{2,1,0:T(8,128)} %copy-done.3, f32[128,16,1024]{2,1,0:T(8,128)} %copy-done.2), kind=kLoop, calls=%fused_computation.19 | loop fusion | flops 3145728 | bytes 25165824 | tf_op jit(solution)/shard_map/add | solution.py:24
  308.4 7.0 pad.108
  315.3 10.2 %pad.109 = f32[32,16,1024]{2,1,0:T(8,128)} pad(f32[16,16,1024]{2,1,0:T(8,128)} %add.263, f32[]{:T(128)} %constant.13.clone.1), padding=1_0_1x0_0_0x0_0_0 | pad | bytes 3145732 | tf_op jit(solution)/shard_map/pad | solution.py:78
  325.5 10.1 %pad.95 = f32[32,16,1024]{2,1,0:T(8,128)} pad(f32[16,16,1024]{2,1,0:T(8,128)} %add.253, f32[]{:T(128)} %constant.13.clone.1), padding=1_0_1x0_0_0x0_0_0 | pad | bytes 3145732 | tf_op jit(solution)/shard_map/pad | solution.py:78
  337.9 10.2 %pad.94 = f32[32,16,1024]{2,1,0:T(8,128)} pad(f32[16,16,1024]{2,1,0:T(8,128)} %pad_maximum_fusion.4, f32[]{:T(128)} %constant.13.clone.1), padding=0_1_1x0_0_0x0_0_0 | pad | bytes 3145732 | tf_op jit(solution)/shard_map/pad | solution.py:78
  362.0 18.6 %pad.96 = f32[64,16,1024]{2,1,0:T(8,128)} pad(f32[32,16,1024]{2,1,0:T(8,128)} %pad_maximum_fusion.2, f32[]{:T(128)} %constant.13.clone.1), padding=0_1_1x0_0_0x0_0_0 | pad | bytes 6291460 | tf_op jit(solution)/shard_map/pad | solution.py:78
  380.6 12.0 %pad.97 = f32[64,16,1024]{2,1,0:T(8,128)} pad(f32[32,16,1024]{2,1,0:T(8,128)S(1)} %copy-done.16, f32[]{:T(128)} %constant.13.clone.1), padding=1_0_1x0_0_0x0_0_0 | pad | bytes 6291460 | tf_op jit(solution)/shard_map/pad | solution.py:78
  392.5 6.8 add.257
  399.4 35.6 %pad.99 = f32[128,16,1024]{2,1,0:T(8,128)} pad(f32[64,16,1024]{2,1,0:T(8,128)} %add.257, f32[]{:T(128)} %constant.13.clone.1), padding=1_0_1x0_0_0x0_0_0 | pad | bytes 12582916 | tf_op jit(solution)/shard_map/pad | solution.py:78
  436.5 18.6 %pad.110 = f32[64,16,1024]{2,1,0:T(8,128)} pad(f32[32,16,1024]{2,1,0:T(8,128)} %pad_maximum_fusion.3, f32[]{:T(128)} %constant.13.clone.1), padding=0_1_1x0_0_0x0_0_0 | pad | bytes 6291460 | tf_op jit(solution)/shard_map/pad | solution.py:78
  455.1 11.9 %pad.111 = f32[64,16,1024]{2,1,0:T(8,128)} pad(f32[32,16,1024]{2,1,0:T(8,128)S(1)} %copy-done.15, f32[]{:T(128)} %constant.13.clone.1), padding=1_0_1x0_0_0x0_0_0 | pad | bytes 6291460 | tf_op jit(solution)/shard_map/pad | solution.py:78
  467.0 7.1 add.265
  475.6 7.6 fusion.12
  485.7 35.5 %pad.98 = f32[128,16,1024]{2,1,0:T(8,128)} pad(f32[64,16,1024]{2,1,0:T(8,128)} %pad_maximum_fusion, f32[]{:T(128)} %constant.13.clone.1), padding=0_1_1x0_0_0x0_0_0 | pad | bytes 12582916 | tf_op jit(solution)/shard_map/pad | solution.py:78
  521.2 35.5 %pad.113 = f32[128,16,1024]{2,1,0:T(8,128)} pad(f32[64,16,1024]{2,1,0:T(8,128)} %add.265, f32[]{:T(128)} %constant.13.clone.1), padding=1_0_1x0_0_0x0_0_0 | pad | bytes 12582916 | tf_op jit(solution)/shard_map/pad | solution.py:78
  561.5 35.5 %pad.112 = f32[128,16,1024]{2,1,0:T(8,128)} pad(f32[64,16,1024]{2,1,0:T(8,128)} %pad_maximum_fusion.1, f32[]{:T(128)} %constant.13.clone.1), padding=0_1_1x0_0_0x0_0_0 | pad | bytes 12582916 | tf_op jit(solution)/shard_map/pad | solution.py:78
  598.8 107.7 %while.11 = (s32[]{:T(128)}, f32[16,1024]{1,0:T(8,128)S(1)}, f32[16,1024]{1,0:T(8,128)S(1)}, f32[16,1024]{1,0:T(8,128)S(1)}, s32[]{:T(128)}, /*index=5*/s32[]{:T(128)}) while((s32[]{:T(128)}, f32[16,1024]{1,0:T(8,128)S(1)}, f32[16,1024]{1,0:T(8,128)S(1)}, f32[16,1024]{1,0:T(8,128)S(1)}, s32[]{:T(128)}, /*index=5*/s32[]{:T(128)}) %tuple.47), condition=%wide.region_4.5_spmd.clone, body=%wide.region_3.4_spmd.clone.sunk | while | flops 81923 | bytes 458871 | solution.py:87
  642.6 6.5 collective-permute-start
  706.5 14.0 %multiply_reduce_fusion = f32[128,1024]{1,0:T(8,128)S(1)} fusion(f32[128,16,1024]{2,1,0:T(8,128)} %pad.112, f32[128,16,1024]{2,1,0:T(8,128)} %pad.113, f32[128,16,1024]{2,1,0:T(8,128)} %pad.98, f32[128,16,1024]{2,1,0:T(8,128)} %pad.99, f32[16,1024]{1,0:T(8,128)S(1)} %get-tuple-element.27, f32[128,16]{1,0:T(8,128)S(1)} %copy-done.28), kind=kLoop, calls=%fused_computation.3 | loop fusion | flops 12451840 | bytes 34152448 | tf_op jit(solution)/shard_map/reduce_sum | solution.py:89
  727.1 39.7 %reduce-scatter.3.cloned.1.call-done = bf16[16,4096]{1,0:T(8,128)(2,1)} async-done(((bf16[128,4096]{1,0:T(8,128)(2,1)}), bf16[16,4096]{1,0:T(8,128)(2,1)}) %reduce-scatter.3.cloned.1.call-update) | async-done | bytes 131088 | tf_op jit(solution)/shard_map/reduce_scatter | solution.py:96
  769.3 16.9 %all_to_all.10 = bf16[16,4,4096]{2,1,0:T(4,128)(2,1)S(1)} all-to-all(bf16[16,4,4096]{2,1,0:T(4,128)(2,1)S(1)} %reshape.78), channel_id=1, replica_groups=mesh['seq'=16,'expert'=8] {'seq'}, dimensions={0} | all-to-all | bytes 1048576 | tf_op jit(solution)/shard_map/all_to_all | solution.py:113
  787.2 29.3 %all-gather.11.cloned.1.call-done = bf16[8,64,4096]{2,1,0:T(8,128)(2,1)} async-done(((bf16[1,64,4096]{2,1,0:T(8,128)(2,1)}), bf16[8,64,4096]{2,1,0:T(8,128)(2,1)}) %all-gather.11.cloned.1.call-update) | async-done | bytes 4194320 | tf_op jit(solution)/shard_map/all_gather | solution.py:116
  816.5 10.1 %fusion.6 = f32[512,896]{1,0:T(8,128)} fusion(bf16[512,4096]{1,0:T(8,128)(2,1)} %bitcast.51, bf16[1,4096,896]{2,1,0:T(8,128)(2,1)} %param.33), kind=kOutput, calls=%fused_computation.9 | convolution fusion | flops 3758096384 | bytes 13369344 | tf_op jit(solution)/shard_map/dot_general | solution.py:119
  826.6 16.7 %fusion.8 = bf16[512,4096]{1,0:T(8,128)(2,1)} fusion(bf16[1,896,4096]{2,1,0:T(8,128)(2,1)} %param.35, f32[512,896]{1,0:T(8,128)} %fusion.6, bf16[512,4096]{1,0:T(8,128)(2,1)} %bitcast.52, bf16[1,4096,896]{2,1,0:T(8,128)(2,1)} %param.34), kind=kOutput, calls=%fused_computation.11 | convolution fusion | flops 7521042432 | bytes 24903680 | tf_op jit(solution)/shard_map/dot_general | solution.py:123
  843.3 38.0 %reduce-scatter.5.cloned.1.call-done = bf16[64,4096]{1,0:T(8,128)(2,1)} async-done(((bf16[512,4096]{1,0:T(8,128)(2,1)}), bf16[64,4096]{1,0:T(8,128)(2,1)}) %reduce-scatter.5.cloned.1.call-update) | async-done | bytes 524304 | tf_op jit(solution)/shard_map/reduce_scatter | solution.py:122
  883.3 7.1 all-to-all-start.1
  890.5 10.1 %all-to-all-done.1 = bf16[16,4,4096]{2,1,0:T(4,128)(2,1)S(1)} async-done(((bf16[16,4,4096]{2,1,0:T(4,128)(2,1)}), bf16[16,4,4096]{2,1,0:T(4,128)(2,1)S(1)}, u32[]{:S(2)}, u32[]{:S(2)}) %all-to-all-start.1) | async-done | bytes 524320 | tf_op jit(solution)/shard_map/all_to_all | solution.py:128
  (257 shorter events, 227.7 us)
Async XLA Ops:
  6.5 155.7 %copy-start = (bf16[1024,288]{0,1:T(8,128)(2,1)S(1)}, bf16[1024,288]{0,1:T(8,128)(2,1)}, u32[]{:S(2)}) copy-start(bf16[1024,288]{0,1:T(8,128)(2,1)} %param.24) | copy-start | bytes 1769476
  6.5 28.4 %all-gather.5.cloned.1.call-start = ((), (), s32[]{:S(2)}) async-start(), calls=%async_computation.4 | async-start | bytes 1179648 | tf_op jit(solution)/shard_map/all_gather | solution.py:49
  7.3 141.1 %all-gather.7.cloned.1.call-start = ((), (), s32[]{:S(2)}) async-start(), calls=%async_computation.5 | async-start | bytes 17825792 | tf_op jit(solution)/shard_map/all_gather | solution.py:55
  8.0 215.6 %all-reduce.30.cloned.1.call-start = ((), (), s32[]{:S(2)}) async-start(), calls=%async_computation.6 | async-start | bytes 131072 | tf_op jit(solution)/shard_map/psum | solution.py:68
  36.4 125.5 %copy-start.39 = (f32[1024]{0:T(1024)S(1)}, f32[1024]{0:T(1024)}, u32[]{:S(2)}) copy-start(f32[1024]{0:T(1024)} %param.23) | copy-start | bytes 12292
  36.4 187.1 %copy-start.42 = (bf16[256,1024]{1,0:T(8,128)(2,1)S(1)}, bf16[256,1024]{1,0:T(8,128)(2,1)}, u32[]{:S(2)}) copy-start(bf16[256,1024]{1,0:T(8,128)(2,1)} %param.25) | copy-start | bytes 1572868
  36.4 187.1 %copy-start.43 = (f32[1024]{0:T(1024)S(1)}, f32[1024]{0:T(1024)}, u32[]{:S(2)}) copy-start(f32[1024]{0:T(1024)} %param.26) | copy-start | bytes 12292
  156.9 68.0 %copy-start.37 = (f32[16,1024]{1,0:T(8,128)S(1)}, f32[16,1024]{1,0:T(8,128)}, u32[]{:S(2)}) copy-start(f32[16,1024]{1,0:T(8,128)} %param.27) | copy-start | bytes 196612
  156.9 5.0 collective-permute-start.1
  162.2 64.8 %copy-start.23 = (bf16[128,1024]{1,0:T(8,128)(2,1)}, bf16[128,1024]{1,0:T(8,128)(2,1)S(1)}, u32[]{:S(2)}) copy-start(bf16[128,1024]{1,0:T(8,128)(2,1)S(1)} %multiply_convert_fusion.1) | copy-start | bytes 786436
  163.2 557.3 %all-gather.9.cloned.1.call-start = ((), (), s32[]{:S(2)}) async-start(), calls=%async_computation.7 | async-start | bytes 8912896 | tf_op jit(solution)/shard_map/all_gather | solution.py:93
  163.8 602.9 %reduce-scatter.3.cloned.1.call-start = ((), (), s32[]{:S(2)}) async-start(), calls=%async_computation.8 | async-start | bytes 1179648 | tf_op jit(solution)/shard_map/reduce_scatter | solution.py:96
  561.5 144.9 %copy-start.28 = (f32[128,16]{1,0:T(8,128)S(1)}, f32[128,16]{1,0:T(8,128)}, u32[]{:S(2)}) copy-start(f32[128,16]{1,0:T(8,128)} %copy.42) | copy-start | bytes 24580
  598.8 5.0 collective-permute-start
  603.9 5.8 collective-permute-start
  609.7 5.9 collective-permute-start
  615.6 5.8 collective-permute-start
  621.5 5.8 collective-permute-start
  627.3 7.2 collective-permute-start
  634.5 8.1 collective-permute-start
  642.6 8.1 collective-permute-start
  650.7 7.9 collective-permute-start
  658.6 7.9 collective-permute-start
  666.6 8.0 collective-permute-start
  674.6 7.8 collective-permute-start
  682.5 7.9 collective-permute-start
  690.4 8.1 collective-permute-start
  698.5 7.9 collective-permute-start
  726.3 90.2 %all-gather.11.cloned.1.call-start = ((), (), s32[]{:S(2)}) async-start(), calls=%async_computation.9 | async-start | bytes 4718592 | tf_op jit(solution)/shard_map/all_gather | solution.py:116
  787.1 94.2 %reduce-scatter.5.cloned.1.call-start = ((), (), s32[]{:S(2)}) async-start(), calls=%async_computation.10 | async-start | bytes 4718592 | tf_op jit(solution)/shard_map/reduce_scatter | solution.py:122
  826.6 75.1 %copy-start.1 = (bf16[1024,288]{0,1:T(8,128)(2,1)S(1)}, bf16[1024,288]{0,1:T(8,128)(2,1)}, u32[]{:S(2)}) copy-start(bf16[1024,288]{0,1:T(8,128)(2,1)} %param.24) | copy-start | bytes 1769476
  883.3 17.2 %all-to-all-start.1 = ((bf16[16,4,4096]{2,1,0:T(4,128)(2,1)}), bf16[16,4,4096]{2,1,0:T(4,128)(2,1)S(1)}, u32[]{:S(2)}, u32[]{:S(2)}) async-start(bf16[16,4,4096]{2,1,0:T(4,128)(2,1)} %reshape.81), calls=%async_computation.3 | async-start | bytes 1048576 | tf_op jit(solution)/shard_map/all_to_all | solution.py:128
  (37 other events, 523.4 us)
Sparse Core Ops, SparseCore 0:
  9.1 25.7 all-gather.4
  37.0 111.3 all-gather.6
  163.4 60.1 all-reduce.29
  225.7 77.5 all-gather.8
  726.4 40.3 reduce-scatter.2
  787.2 29.2 all-gather.10
  843.4 37.8 reduce-scatter.4
where the time goes:
time: 924 us; the launch traced here: 909 us
  waiting for transfers between devices  327 us (35%)
  local copies, waits for them, and re-layouts  289 us (31%)
  other arithmetic  109 us (12%)
  starting transfers between devices  94.2 us (10%)
  matrix products  44.8 us (5%)
  blocking collectives  30.9 us (3%)
  between operations  14 us (2%)
    pad x24, local copies, waits for them, and re-layouts, per_device(): lax.associative_scan(combine_states, (decay, source), axis=0)  267 us
    all_gather x1, waiting for transfers between devices, per_device(): lax.all_gather(in_weight, 'seq', axis=1, tiled=True)  112 us
    ppermute x16, starting transfers between devices, from_behind(): return lax.ppermute(block, axis, route)  86.9 us
    psum x1, waiting for transfers between devices, per_device(): lax.psum(partial_value[:, :RANK].astype(jnp.bfloat16), 'expert')  44.8 us
    reduce_scatter x1, waiting for transfers between devices, per_device(): lax.psum_scatter(terms.astype(jnp.bfloat16), 'expert', scatter_dimension=...  39.7 us
    reduce_scatter x1, waiting for transfers between devices, per_device(): lax.psum_scatter(jnp.dot(act, w_down[0], preferred_element_type=jnp.float...  38 us
    add x12, other arithmetic, combine_states(): return (earlier[0] * later[0], later[0] * earlier[1] + later[1])  34.6 us
    add x12, other arithmetic, per_device(): lax.associative_scan(combine_states, (decay, source), axis=0)  33.2 us
  transfers between devices with their start and end apart: 24, of which 23 were waited for; matrix products, arithmetic and copies ran while one was open for 42% of the time, Pallas kernels for 0%

commit v1 on v0

--- a/solution.py
+++ b/solution.py
@@ -46,7 +46,14 @@
     rows, dim = tokens.shape
     n_seq = lax.axis_size("seq")
     n_exp = lax.axis_size("expert")
-    group = lax.all_gather(tokens, "expert", axis=0, tiled=True)
+    ring = [tokens]
+    for hop in range(7):
+        ring.append(lax.ppermute(ring[-1], "expert", [(dev, (dev + 1) % 8) for dev in range(8)]))
+    group = jnp.roll(
+        jnp.concatenate(ring[::-1], axis=0),
+        (lax.axis_index("expert") + 1) * ring[0].shape[0],
+        axis=0,
+    )
     local_tok = group.shape[0]
     normed = rms_norm(group, gain_mamba).astype(jnp.bfloat16)
     both = jnp.einsum(

time: 924 us -> 896 us (0.970)
  waiting for transfers between devices: 327 us -> 302 us
    ppermute x0 -> x7, waiting for transfers between devices: none -> 38.5 us  [per_device(): lax.ppermute(ring[-1], 'expert', [(dev, (dev + 1) % 8) for dev in range(8)])]
    all_gather x1, waiting for transfers between devices: 112 us -> 75.1 us  [per_device(): lax.all_gather(in_weight, 'seq', axis=1, tiled=True)]
    all_gather x1 -> x0, waiting for transfers between devices: 26 us -> none  [per_device(): group = lax.all_gather(tokens, 'expert', axis=0, tiled=True)]
  transfers between devices with their start and end apart: 24 -> 30, of which waited for: 23 -> 29; matrix products, arithmetic and copies ran while one was open for 42% -> 43% of each run, Pallas kernels for 0% -> 0%
where the time goes in v1:
time: 896 us; the launch traced here: 881 us
  waiting for transfers between devices  302 us (34%)
  local copies, waits for them, and re-layouts  291 us (32%)
  other arithmetic  104 us (12%)
  starting transfers between devices  94.3 us (11%)
  matrix products  44.4 us (5%)
  blocking collectives  30.9 us (3%)
  between operations  14.2 us (2%)
    pad x24, local copies, waits for them, and re-layouts, per_device(): lax.associative_scan(combine_states, (decay, source), axis=0)  266 us
    ppermute x16, starting transfers between devices, from_behind(): return lax.ppermute(block, axis, route)  87 us
    all_gather x1, waiting for transfers between devices, per_device(): lax.all_gather(in_weight, 'seq', axis=1, tiled=True)  75.1 us
    psum x1, waiting for transfers between devices, per_device(): lax.psum(partial_value[:, :RANK].astype(jnp.bfloat16), 'expert')  44.7 us
    reduce_scatter x1, waiting for transfers between devices, per_device(): lax.psum_scatter(terms.astype(jnp.bfloat16), 'expert', scatter_dimension=...  39.7 us
    ppermute x7, waiting for transfers between devices, per_device(): lax.ppermute(ring[-1], 'expert', [(dev, (dev + 1) % 8) for dev in range(8)])  38.5 us
    reduce_scatter x1, waiting for transfers between devices, per_device(): lax.psum_scatter(jnp.dot(act, w_down[0], preferred_element_type=jnp.float...  38 us
    add x12, other arithmetic, combine_states(): return (earlier[0] * later[0], later[0] * earlier[1] + later[1])  32.8 us
  transfers between devices with their start and end apart: 30, of which 29 were waited for; matrix products, arithmetic and copies ran while one was open for 43% of the time, Pallas kernels for 0%

profile of v1, /device:TPU:0, one launch (start us, length us, event | category | flops | bytes accessed | tf_op | source)
XLA Modules:
  0.0 880.8 jit_solution(14474350114319503244)
XLA Ops:
  48.4 75.1 %all-gather.4.cloned.1.call-done = bf16[2,4096,1024]{2,1,0:T(8,128)(2,1)} async-done(((bf16[2,256,1024]{2,1,0:T(8,128)(2,1)}), bf16[2,4096,1024]{2,1,0:T(8,128)(2,1)}) %all-gather.4.cloned.1.call-update) | async-done | bytes 16777232 | tf_op jit(solution)/shard_map/all_gather | solution.py:62
  123.4 8.1 fusion.20
  138.8 14.0 %psum.14 = bf16[128,32]{0,1:T(8,128)(2,1)S(1)} all-reduce(bf16[128,32]{0,1:T(8,128)(2,1)S(1)} %slice.341), channel_id=1, replica_groups=mesh['seq'=16,'expert'=8] {'expert'}, use_global_device_ids=true, to_apply=%region_1.2 | all-reduce | flops 4096 | bytes 16384 | tf_op jit(solution)/shard_map/psum | solution.py:76
  153.6 44.7 %all-reduce.30.cloned.1.call-done = bf16[128,256]{0,1:T(8,128)(2,1)} async-done(((bf16[128,256]{0,1:T(8,128)(2,1)}), bf16[128,256]{0,1:T(8,128)(2,1)}) %all-reduce.30.cloned.1.call-update) | async-done | bytes 65552 | tf_op jit(solution)/shard_map/psum | solution.py:75
  208.2 10.9 %slice_add_fusion = (f32[64,16,1024]{2,1,0:T(8,128)S(1)}, f32[64,16,1024]{2,1,0:T(8,128)}) fusion(f32[128,16,1024]{2,1,0:T(8,128)} %copy-done.3, f32[128,16,1024]{2,1,0:T(8,128)} %copy-done.2), kind=kLoop, calls=%fused_computation.19 | loop fusion | flops 3145728 | bytes 25165824 | tf_op jit(solution)/shard_map/add | solution.py:24
  280.7 7.0 pad.108
  287.7 10.2 %pad.109 = f32[32,16,1024]{2,1,0:T(8,128)} pad(f32[16,16,1024]{2,1,0:T(8,128)} %add.279, f32[]{:T(128)} %constant.56.clone.1), padding=1_0_1x0_0_0x0_0_0 | pad | bytes 3145732 | tf_op jit(solution)/shard_map/pad | solution.py:85
  297.9 10.1 %pad.95 = f32[32,16,1024]{2,1,0:T(8,128)} pad(f32[16,16,1024]{2,1,0:T(8,128)} %add.269, f32[]{:T(128)} %constant.56.clone.1), padding=1_0_1x0_0_0x0_0_0 | pad | bytes 3145732 | tf_op jit(solution)/shard_map/pad | solution.py:85
  310.2 10.1 %pad.94 = f32[32,16,1024]{2,1,0:T(8,128)} pad(f32[16,16,1024]{2,1,0:T(8,128)} %pad_maximum_fusion.4, f32[]{:T(128)} %constant.56.clone.1), padding=0_1_1x0_0_0x0_0_0 | pad | bytes 3145732 | tf_op jit(solution)/shard_map/pad | solution.py:85
  334.2 18.6 %pad.96 = f32[64,16,1024]{2,1,0:T(8,128)} pad(f32[32,16,1024]{2,1,0:T(8,128)} %pad_maximum_fusion.2, f32[]{:T(128)} %constant.56.clone.1), padding=0_1_1x0_0_0x0_0_0 | pad | bytes 6291460 | tf_op jit(solution)/shard_map/pad | solution.py:85
  352.8 11.9 %pad.97 = f32[64,16,1024]{2,1,0:T(8,128)} pad(f32[32,16,1024]{2,1,0:T(8,128)S(1)} %copy-done.16, f32[]{:T(128)} %constant.56.clone.1), padding=1_0_1x0_0_0x0_0_0 | pad | bytes 6291460 | tf_op jit(solution)/shard_map/pad | solution.py:85
  364.7 6.9 add.273
  371.6 35.6 %pad.99 = f32[128,16,1024]{2,1,0:T(8,128)} pad(f32[64,16,1024]{2,1,0:T(8,128)} %add.273, f32[]{:T(128)} %constant.56.clone.1), padding=1_0_1x0_0_0x0_0_0 | pad | bytes 12582916 | tf_op jit(solution)/shard_map/pad | solution.py:85
  408.7 18.6 %pad.110 = f32[64,16,1024]{2,1,0:T(8,128)} pad(f32[32,16,1024]{2,1,0:T(8,128)} %pad_maximum_fusion.3, f32[]{:T(128)} %constant.56.clone.1), padding=0_1_1x0_0_0x0_0_0 | pad | bytes 6291460 | tf_op jit(solution)/shard_map/pad | solution.py:85
  427.2 11.9 %pad.111 = f32[64,16,1024]{2,1,0:T(8,128)} pad(f32[32,16,1024]{2,1,0:T(8,128)S(1)} %copy-done.15, f32[]{:T(128)} %constant.56.clone.1), padding=1_0_1x0_0_0x0_0_0 | pad | bytes 6291460 | tf_op jit(solution)/shard_map/pad | solution.py:85
  439.2 7.1 add.281
  447.8 7.5 fusion.12
  457.9 35.5 %pad.98 = f32[128,16,1024]{2,1,0:T(8,128)} pad(f32[64,16,1024]{2,1,0:T(8,128)} %pad_maximum_fusion, f32[]{:T(128)} %constant.56.clone.1), padding=0_1_1x0_0_0x0_0_0 | pad | bytes 12582916 | tf_op jit(solution)/shard_map/pad | solution.py:85
  493.4 35.5 %pad.113 = f32[128,16,1024]{2,1,0:T(8,128)} pad(f32[64,16,1024]{2,1,0:T(8,128)} %add.281, f32[]{:T(128)} %constant.56.clone.1), padding=1_0_1x0_0_0x0_0_0 | pad | bytes 12582916 | tf_op jit(solution)/shard_map/pad | solution.py:85
  533.8 35.5 %pad.112 = f32[128,16,1024]{2,1,0:T(8,128)} pad(f32[64,16,1024]{2,1,0:T(8,128)} %pad_maximum_fusion.1, f32[]{:T(128)} %constant.56.clone.1), padding=0_1_1x0_0_0x0_0_0 | pad | bytes 12582916 | tf_op jit(solution)/shard_map/pad | solution.py:85
  571.1 107.7 %while.11 = (s32[]{:T(128)}, f32[16,1024]{1,0:T(8,128)S(1)}, f32[16,1024]{1,0:T(8,128)S(1)}, f32[16,1024]{1,0:T(8,128)S(1)}, s32[]{:T(128)}, /*index=5*/s32[]{:T(128)}) while((s32[]{:T(128)}, f32[16,1024]{1,0:T(8,128)S(1)}, f32[16,1024]{1,0:T(8,128)S(1)}, f32[16,1024]{1,0:T(8,128)S(1)}, s32[]{:T(128)}, /*index=5*/s32[]{:T(128)}) %tuple.47), condition=%wide.region_4.5_spmd.clone, body=%wide.region_3.4_spmd.clone.sunk | while | flops 81923 | bytes 458871 | solution.py:94
  606.8 6.5 collective-permute-start
  662.7 6.5 collective-permute-start
  678.8 14.0 %multiply_reduce_fusion = f32[128,1024]{1,0:T(8,128)S(1)} fusion(f32[128,16,1024]{2,1,0:T(8,128)} %pad.112, f32[128,16,1024]{2,1,0:T(8,128)} %pad.113, f32[128,16,1024]{2,1,0:T(8,128)} %pad.98, f32[128,16,1024]{2,1,0:T(8,128)} %pad.99, f32[16,1024]{1,0:T(8,128)S(1)} %get-tuple-element.27, f32[128,16]{1,0:T(8,128)S(1)} %copy-done.31), kind=kLoop, calls=%fused_computation.3 | loop fusion | flops 12451840 | bytes 34152448 | tf_op jit(solution)/shard_map/reduce_sum | solution.py:96
  699.4 39.7 %reduce-scatter.3.cloned.1.call-done = bf16[16,4096]{1,0:T(8,128)(2,1)} async-done(((bf16[128,4096]{1,0:T(8,128)(2,1)}), bf16[16,4096]{1,0:T(8,128)(2,1)}) %reduce-scatter.3.cloned.1.call-update) | async-done | bytes 131088 | tf_op jit(solution)/shard_map/reduce_scatter | solution.py:103
  741.6 16.9 %all_to_all.10 = bf16[16,4,4096]{2,1,0:T(4,128)(2,1)S(1)} all-to-all(bf16[16,4,4096]{2,1,0:T(4,128)(2,1)S(1)} %reshape.78), channel_id=1, replica_groups=mesh['seq'=16,'expert'=8] {'seq'}, dimensions={0} | all-to-all | bytes 1048576 | tf_op jit(solution)/shard_map/all_to_all | solution.py:120
  759.6 29.3 %all-gather.8.cloned.1.call-done = bf16[8,64,4096]{2,1,0:T(8,128)(2,1)} async-done(((bf16[1,64,4096]{2,1,0:T(8,128)(2,1)}), bf16[8,64,4096]{2,1,0:T(8,128)(2,1)}) %all-gather.8.cloned.1.call-update) | async-done | bytes 4194320 | tf_op jit(solution)/shard_map/all_gather | solution.py:123
  788.9 10.1 %fusion.6 = f32[512,896]{1,0:T(8,128)} fusion(bf16[512,4096]{1,0:T(8,128)(2,1)} %bitcast.51, bf16[1,4096,896]{2,1,0:T(8,128)(2,1)} %param.33), kind=kOutput, calls=%fused_computation.9 | convolution fusion | flops 3758096384 | bytes 13369344 | tf_op jit(solution)/shard_map/dot_general | solution.py:126
  798.9 16.6 %fusion.8 = bf16[512,4096]{1,0:T(8,128)(2,1)} fusion(bf16[1,896,4096]{2,1,0:T(8,128)(2,1)} %param.35, f32[512,896]{1,0:T(8,128)} %fusion.6, bf16[512,4096]{1,0:T(8,128)(2,1)} %bitcast.52, bf16[1,4096,896]{2,1,0:T(8,128)(2,1)} %param.34), kind=kOutput, calls=%fused_computation.11 | convolution fusion | flops 7521042432 | bytes 24903680 | tf_op jit(solution)/shard_map/dot_general | solution.py:130
  815.6 38.0 %reduce-scatter.5.cloned.1.call-done = bf16[64,4096]{1,0:T(8,128)(2,1)} async-done(((bf16[512,4096]{1,0:T(8,128)(2,1)}), bf16[64,4096]{1,0:T(8,128)(2,1)}) %reduce-scatter.5.cloned.1.call-update) | async-done | bytes 524304 | tf_op jit(solution)/shard_map/reduce_scatter | solution.py:129
  855.7 7.1 all-to-all-start.1
  862.8 10.1 %all-to-all-done.1 = bf16[16,4,4096]{2,1,0:T(4,128)(2,1)S(1)} async-done(((bf16[16,4,4096]{2,1,0:T(4,128)(2,1)}), bf16[16,4,4096]{2,1,0:T(4,128)(2,1)S(1)}, u32[]{:S(2)}, u32[]{:S(2)}) %all-to-all-start.1) | async-done | bytes 524320 | tf_op jit(solution)/shard_map/all_to_all | solution.py:135
  (292 shorter events, 256.9 us)
Async XLA Ops:
  6.5 130.4 %copy-start = (bf16[1024,288]{0,1:T(8,128)(2,1)S(1)}, bf16[1024,288]{0,1:T(8,128)(2,1)}, u32[]{:S(2)}) copy-start(bf16[1024,288]{0,1:T(8,128)(2,1)} %param.24) | copy-start | bytes 1769476
  6.5 116.9 %all-gather.4.cloned.1.call-start = ((), (), s32[]{:S(2)}) async-start(), calls=%async_computation.4 | async-start | bytes 17825792 | tf_op jit(solution)/shard_map/all_gather | solution.py:62
  7.3 191.0 %all-reduce.30.cloned.1.call-start = ((), (), s32[]{:S(2)}) async-start(), calls=%async_computation.5 | async-start | bytes 131072 | tf_op jit(solution)/shard_map/psum | solution.py:75
  7.3 5.8 collective-permute-start.1
  13.1 5.6 collective-permute-start.2
  18.7 5.6 collective-permute-start.3
  24.3 5.6 collective-permute-start.4
  29.9 5.6 collective-permute-start.5
  35.5 5.6 collective-permute-start.6
  41.2 5.6 collective-permute-start.7
  131.6 5.0 collective-permute-start.8
  138.0 554.9 %all-gather.6.cloned.1.call-start = ((), (), s32[]{:S(2)}) async-start(), calls=%async_computation.6 | async-start | bytes 8912896 | tf_op jit(solution)/shard_map/all_gather | solution.py:100
  138.7 600.4 %reduce-scatter.3.cloned.1.call-start = ((), (), s32[]{:S(2)}) async-start(), calls=%async_computation.7 | async-start | bytes 1179648 | tf_op jit(solution)/shard_map/reduce_scatter | solution.py:103
  569.3 109.5 %copy-start.31 = (f32[128,16]{1,0:T(8,128)S(1)}, f32[128,16]{1,0:T(8,128)}, u32[]{:S(2)}) copy-start(f32[128,16]{1,0:T(8,128)} %copy.42) | copy-start | bytes 24580
  571.1 5.0 collective-permute-start
  576.2 5.8 collective-permute-start
  582.0 6.0 collective-permute-start
  588.0 5.8 collective-permute-start
  593.8 5.8 collective-permute-start
  599.7 7.1 collective-permute-start
  606.8 8.1 collective-permute-start
  614.9 8.1 collective-permute-start
  623.0 7.9 collective-permute-start
  630.9 7.9 collective-permute-start
  638.9 8.0 collective-permute-start
  646.9 7.8 collective-permute-start
  654.8 8.0 collective-permute-start
  662.7 8.1 collective-permute-start
  670.9 7.9 collective-permute-start
  698.6 90.3 %all-gather.8.cloned.1.call-start = ((), (), s32[]{:S(2)}) async-start(), calls=%async_computation.8 | async-start | bytes 4718592 | tf_op jit(solution)/shard_map/all_gather | solution.py:123
  759.5 94.1 %reduce-scatter.5.cloned.1.call-start = ((), (), s32[]{:S(2)}) async-start(), calls=%async_computation.9 | async-start | bytes 4718592 | tf_op jit(solution)/shard_map/reduce_scatter | solution.py:129
  855.7 17.2 %all-to-all-start.1 = ((bf16[16,4,4096]{2,1,0:T(4,128)(2,1)}), bf16[16,4,4096]{2,1,0:T(4,128)(2,1)S(1)}, u32[]{:S(2)}, u32[]{:S(2)}) async-start(bf16[16,4,4096]{2,1,0:T(4,128)(2,1)} %reshape.81), calls=%async_computation.3 | async-start | bytes 1048576 | tf_op jit(solution)/shard_map/all_to_all | solution.py:135
  (47 other events, 969.1 us)
Sparse Core Ops, SparseCore 0:
  9.5 113.8 all-gather.3
  138.1 60.1 all-reduce.29
  200.6 77.5 all-gather.5
  698.7 40.3 reduce-scatter.2
  759.6 29.1 all-gather.7
  815.7 37.8 reduce-scatter.4
